TPU v7x, 512 devices: a whole 4x8x8 slice. The times are simulated.
512 devices in a mesh: seq: 64 (over x, y, core), head: 8 (over z).
Axes of the slice: x: 4, y: 8, z: 8, core: 2. Of those that a mesh axis runs over, the one named last changes fastest.
Arguments:
- queries: bfloat16 [128, 8192], P('seq', 'head'), may hold values from -12 to 12
- prefix_keys: bfloat16 [262144, 1024], P('seq', 'head'), may hold values from -6 to 6
- prefix_values: bfloat16 [262144, 1024], P('seq', 'head'), may hold values from -12 to 12
- suffix_keys: bfloat16 [128, 2048, 1024], P('seq', None, 'head'), may hold values from -8.375 to 8.375
- suffix_values: bfloat16 [128, 2048, 1024], P('seq', None, 'head'), may hold values from -12 to 12
- suffix_length: int32 [128], P('seq'), may hold values from 1 to 2048, 131072 in all
- slot_answer: int32 [128], P('seq'), may hold values from 0 to 127, each once
Outputs:
- attended: bfloat16 [128, 8192], P('seq')
Inputs may be any that keep to these rules, and one draw needn't show every extreme that they name: `suffix_length`: the longest suffix has exactly 2048 live positions. `slot_answer`: every answer is held by exactly one slot.
All inputs are finite; a program needn't handle non-finite values. No bound on the sum of `suffix_length` on one device may be relied on, other than what follows from the above.
Results may differ from a plain program's by a relative error of at most 0.005.
Values may be sent and summed in bfloat16 or wider, within the bound.
A program may use at most 64 MiB of HBM per device.

v0:
```python
import math

import jax
import jax.numpy as jnp
from jax import lax
from jax.sharding import PartitionSpec as P

QH = 64
KVH = 8
HD = 128


NEG_BIG = -1e30


def prefix_part(query_rows, key_block, value_block, score_scale):
    row_count = query_rows.shape[0]
    block_rows = 512
    stacked = query_rows.reshape(row_count // block_rows, block_rows, query_rows.shape[1])

    def one_block(row_block):
        scores = (
            lax.dot_general(
                row_block, key_block, (((1,), (1,)), ((), ())), preferred_element_type=jnp.float32
            )
            * score_scale
        )
        row_top = jnp.max(scores, axis=1)
        weights = jnp.exp(scores - row_top[:, None])
        row_total = jnp.sum(weights, axis=1)
        summed = jnp.dot(
            weights.astype(jnp.bfloat16), value_block, preferred_element_type=jnp.float32
        )
        return (row_top, row_total, summed)

    tops, totals, sums = lax.map(one_block, stacked)
    return (
        tops.reshape(row_count),
        totals.reshape(row_count),
        sums.reshape(row_count, value_block.shape[1]),
    )


def on_device(
    queries, prefix_keys, prefix_values, suffix_keys, suffix_values, suffix_length, slot_answer
):
    head_dim = HD
    per_group = QH // KVH
    score_scale = 1.0 / math.sqrt(head_dim)
    gathered = lax.all_gather(queries, "seq", axis=0, tiled=True)
    answers = gathered.shape[0]
    slots = slot_answer.shape[0]
    suffix_cap = suffix_keys.shape[1]
    onehot = (slot_answer[:, None] == jnp.arange(answers, dtype=jnp.int32)[None, :]).astype(
        jnp.float32
    )
    live_mask = jnp.arange(suffix_cap, dtype=jnp.int32)[None, :] < suffix_length[:, None]
    slot_queries = jnp.take(gathered, slot_answer, axis=0)
    top_parts, total_parts, sum_parts = ([], [], [])
    query_rows = gathered.reshape(answers * per_group, head_dim)
    pre_top, pre_total, pre_sum = prefix_part(query_rows, prefix_keys, prefix_values, score_scale)
    pre_top = pre_top.reshape(answers, per_group)
    pre_total = pre_total.reshape(answers, per_group)
    pre_sum = pre_sum.reshape(answers, per_group, head_dim)
    slot_query = slot_queries.reshape(slots, per_group, head_dim)
    slot_scores = (
        jnp.einsum("ahd,akd->ahk", slot_query, suffix_keys, preferred_element_type=jnp.float32)
        * score_scale
    )
    slot_scores = jnp.where(live_mask[:, None, :], slot_scores, NEG_BIG)
    slot_top = jnp.max(slot_scores, axis=2)
    slot_weights = jnp.where(
        live_mask[:, None, :], jnp.exp(slot_scores - slot_top[:, :, None]), 0.0
    )
    slot_total = jnp.sum(slot_weights, axis=2)
    slot_sum = jnp.einsum(
        "ahk,akd->ahd",
        slot_weights.astype(jnp.bfloat16),
        suffix_values,
        preferred_element_type=jnp.float32,
    )
    spread_top = jnp.max(jnp.where(onehot[:, :, None] > 0.5, slot_top[:, None, :], NEG_BIG), axis=0)
    local_top = jnp.maximum(pre_top, spread_top)
    pre_factor = jnp.exp(pre_top - local_top)
    slot_factor = jnp.exp(slot_top - jnp.take(local_top, slot_answer, axis=0))
    moved_total = lax.dot_general(
        onehot, slot_total * slot_factor, (((0,), (0,)), ((), ())), precision=lax.Precision.HIGHEST
    )
    moved_sum = lax.dot_general(
        onehot,
        (slot_sum * slot_factor[:, :, None]).reshape(slots, per_group * head_dim),
        (((0,), (0,)), ((), ())),
        precision=lax.Precision.HIGHEST,
    )
    top_parts.append(local_top)
    total_parts.append(pre_total * pre_factor + moved_total)
    sum_parts.append(
        pre_sum * pre_factor[:, :, None] + moved_sum.reshape(answers, per_group, head_dim)
    )
    row_tops = top_parts[0]
    row_totals = total_parts[0]
    row_sums = sum_parts[0]
    overall = lax.pmax(row_tops, "seq")
    factor = jnp.exp(row_tops - overall)
    own_sum, own_total = (
        lax.psum_scatter(row_sums * factor[:, :, None], "seq", scatter_dimension=0, tiled=True),
        lax.psum_scatter(row_totals * factor, "seq", scatter_dimension=0, tiled=True),
    )
    result = (own_sum / own_total[:, :, None]).astype(jnp.bfloat16)
    result = result.reshape(own_sum.shape[0], own_sum.shape[1] * head_dim)
    return lax.all_gather(result, "head", axis=1, tiled=True)


def solution(mesh):
    in_specs = (
        P("seq", "head"),
        P("seq", "head"),
        P("seq", "head"),
        P("seq", None, "head"),
        P("seq", None, "head"),
        P("seq"),
        P("seq"),
    )
    out_specs = P("seq", None)
    return jax.shard_map(
        on_device, mesh=mesh, in_specs=in_specs, out_specs=out_specs, check_vma=False
    )
```

profile of v0, /device:TPU:64, one launch (start us, length us, event | category | flops | bytes accessed | tf_op | source)
XLA Modules:
  0.0 481.5 jit_solution(6572474292301644321)
XLA Ops:
  6.5 0.0 copy-start
  6.5 0.0 reduce-scatter.2.cloned.1.call-start
  6.5 0.7 compare_select_fusion
  7.3 0.7 compare_and_fusion
  7.9 0.7 convert_compare_fusion
  8.7 39.8 %all-gather = bf16[64,2,1024]{2,1,0:T(2,128)(2,1)S(1)} all-gather(bf16[1,2,1024]{2,1,0:T(2,128)(2,1)} %bitcast.58), channel_id=1, replica_groups=mesh['seq'=64,'head'=8] {'seq'}, dimensions={0}, use_global_device_ids=true | all-gather | bytes 266240 | tf_op jit(solution)/shard_map/all_gather | solution.py:50
  48.5 0.1 reshape.119
  48.6 0.2 reshape_reshape.12
  48.8 0.7 iota_compare_fusion
  49.6 0.0 copy-start.2
  49.6 0.0 copy-start.3
  49.6 12.9 %while.14 = (s32[]{:T(128)}, f32[2,512]{1,0:T(2,128)S(1)}, f32[2,512]{1,0:T(2,128)S(1)}, f32[2,512,128]{2,1,0:T(8,128)}, bf16[2,512,128]{2,1,0:T(8,128)(2,1)S(1)...) while((s32[]{:T(128)}, f32[2,512]{1,0:T(2,128)S(1)}, ...), condition=%wide.region_3.4_spmd, body=%wide.region_0.3_spmd.sunk | while | flops 1090518016 | bytes 31867524 | solution.py:36
  49.6 0.0 copy-start.1
  49.6 2.7 multiply_reduce_fusion.2
  52.3 0.0 copy-done.1
  52.3 2.1 fusion.50
  54.5 1.5 fusion.49
  56.1 0.0 copy-start.1
  56.1 2.7 multiply_reduce_fusion.2
  58.8 0.0 copy-done.1
  58.8 2.2 fusion.50
  60.9 1.5 fusion.49
  62.5 0.1 reshape_reshape.14
  62.6 0.6 gather_fusion
  63.2 0.0 copy-done
  63.2 0.5 fusion.36
  63.7 0.1 select_reduce_fusion
  63.8 126.9 %pmax.7 = f32[128,8]{0,1:T(8,128)S(1)} all-reduce(f32[128,8]{0,1:T(8,128)S(1)} %get-tuple-element.62), channel_id=1, replica_groups=mesh['seq'=64,'head'=8] {'seq'}, use_global_device_ids=true, to_apply=%region_6.7 | all-reduce | flops 1024 | bytes 8192 | tf_op jit(solution)/shard_map/pmax | solution.py:103
  190.7 0.1 copy.27
  190.8 0.6 gather_fusion.1
  191.4 0.1 subtract_exponential_fusion.3
  191.5 0.0 copy-done.2
  191.5 0.3 fusion.17
  191.8 0.0 copy-done.3
  191.8 1.7 fusion.16
  193.5 1.1 copy.28
  194.6 0.0 reduce-scatter.2.cloned.1.call-update
  194.6 0.1 reshape_reshape.15
  194.8 0.2 fusion.19
  195.0 0.2 fusion.18
  195.2 0.1 copy.31
  195.3 1.3 dynamic-slice
  197.2 246.2 %all-reduce = f32[128,8]{1,0:T(8,128)S(1)} all-reduce(f32[128,8]{1,0:T(8,128)S(1)} %copy.31), channel_id=3, replica_groups=mesh['seq'=64,'head'=8] {'seq'}, use_global_device_ids=true, to_apply=%region_9.10.clone | all-reduce | flops 1024 | bytes 8192
  443.4 0.0 reduce-scatter.2.cloned.1.call-done
  443.4 0.8 fusion.27
  444.2 29.9 %all_gather.7 = bf16[2,8192]{1,0:T(2,128)(2,1)S(1)} all-gather(bf16[2,1024]{1,0:T(2,128)(2,1)S(1)} %bitcast.57), channel_id=1, replica_groups=mesh['seq'=64,'head'=8] {'head'}, dimensions={1}, use_global_device_ids=true | all-gather | bytes 36864 | tf_op jit(solution)/shard_map/all_gather | solution.py:111
  474.1 0.6 copy.67
  (14 shorter events, 0.3 us)
Async XLA Ops:
  6.5 56.7 %copy-start = (bf16[2,2048,128]{2,1,0:T(8,128)(2,1)S(1)}, bf16[2,2048,128]{2,1,0:T(8,128)(2,1)}, u32[]{:S(2)}) copy-start(bf16[2,2048,128]{2,1,0:T(8,128)(2,1)} %param.12) | copy-start | bytes 3145732
  6.5 436.9 %reduce-scatter.2.cloned.1.call-start = ((), (), s32[]{:S(2)}) async-start(), calls=%async_computation.1 | async-start | bytes 532480 | tf_op jit(solution)/shard_map/reduce_scatter | solution.py:106
  49.6 141.9 %copy-start.2 = (bf16[2,2048,128]{2,1,0:T(8,128)(2,1)S(1)}, bf16[2,2048,128]{2,1,0:T(8,128)(2,1)}, u32[]{:S(2)}) copy-start(bf16[2,2048,128]{2,1,0:T(8,128)(2,1)} %param.13) | copy-start | bytes 3145732
  49.6 142.2 %copy-start.3 = (s32[2]{0:T(128)S(1)}, s32[2]{0:T(128)}, u32[]{:S(2)}) copy-start(s32[2]{0:T(128)} %param.15) | copy-start | bytes 28
  49.6 2.7 copy-start.1
  56.1 2.7 copy-start.1
Sparse Core Ops, SparseCore 0:
  194.7 143.1 reduce-scatter.1
where the time goes:
time: 482 us
  blocking collectives  443 us (92%)
  between operations  14.2 us (3%)
  matrix products  12.4 us (3%)
  other arithmetic  7.02 us (1%)
  local copies, waits for them, and re-layouts  5.1 us (1%)
    unnamed x1, blocking collectives  246 us
    pmax x1, blocking collectives, on_device(): overall = lax.pmax(row_tops, 'seq')  127 us
    all_gather x1, blocking collectives, on_device(): gathered = lax.all_gather(queries, 'seq', axis=0, tiled=True)  39.8 us
    all_gather x1, blocking collectives, on_device(): return lax.all_gather(result, 'head', axis=1, tiled=True)  29.9 us
  transfers between devices with their start and end apart: 1, of which 0 were waited for; matrix products, arithmetic and copies ran while one was open for 0% of the time, Pallas kernels for 0%

commit v1 on v0

v1 whole, which is shorter than its diff:
```python
import functools
import math

import jax
import jax.numpy as jnp
from jax import lax
from jax.experimental import pallas as pl
from jax.experimental.pallas import tpu as pltpu
from jax.sharding import PartitionSpec as P

HD = 128
PER_GROUP = 8
NEG_BIG = -1e30
EXP2_SCALE = math.log2(math.e) / math.sqrt(HD)
ROWS = 16
F32 = jnp.float32
BF16 = jnp.bfloat16
MESH = pl.DeviceIdType.MESH


def attend(x_chips, y_chips, z_chips, chunk, q_ref, pk, pv, sk, sv, slen, sans, out_ref, qbuf, kraw, kt, vbuf, skb, svb,
           sbuf, own, give, take, slot, msg, got, zbuf, local_sem, qsend, qrecv, fsend, frecv, psend, precv, msend, mrecv, zsend, zrecv):
    seq, z = lax.axis_index("seq"), lax.axis_index("head")
    core, chip = seq % 2, seq // 2
    x, y = chip // y_chips, chip % y_chips
    sibling = chip * 2 + 1 - core
    chips = x_chips * y_chips
    unit_rows = y_chips * ROWS
    keys = kraw.shape[0]

    def device(xx, yy):
        return (xx * y_chips + yy) * 2 + core

    copies = [
        pltpu.make_async_copy(pk, kraw, local_sem.at[0]),
        pltpu.make_async_copy(pv, vbuf, local_sem.at[1]),
        pltpu.make_async_copy(sk, skb, local_sem.at[2]),
        pltpu.make_async_copy(sv, svb, local_sem.at[3]),
        pltpu.make_async_copy(q_ref, qbuf.at[y], local_sem.at[4]),
    ]

    barrier = pltpu.get_barrier_semaphore()
    pl.semaphore_signal(barrier, inc=1, device_id=(sibling, z), device_id_type=MESH)

    @pl.loop(1, chips)
    def _(step):
        pl.semaphore_signal(barrier, inc=1, device_id=((chip + step) % chips * 2 + core, z), device_id_type=MESH)

    @pl.loop(1, z_chips)
    def _(step):
        pl.semaphore_signal(barrier, inc=1, device_id=(seq, (z + step) % z_chips), device_id_type=MESH)

    for copy in copies:
        copy.start()
    pl.semaphore_wait(barrier, 1 + (chips - 1) + (z_chips - 1))

    def send_queries(group, step):
        return pltpu.make_async_remote_copy(
            src_ref=q_ref,
            dst_ref=qbuf.at[group * y_chips + y],
            send_sem=qsend,
            recv_sem=qrecv.at[group],
            device_id=(device((x + x_chips - group) % x_chips, (y + step) % y_chips), z),
            device_id_type=MESH,
        )

    for group in range(x_chips):

        @pl.loop(1 if group == 0 else 0, y_chips)
        def _(step, group=group):
            send_queries(group, step).start()

    copies[0].wait()

    @pl.loop(0, keys // chunk)
    def _(step):
        at = pl.multiple_of(step * chunk, chunk)
        kt[:, pl.ds(at, chunk)] = kraw[pl.ds(at, chunk), :].T

    copies[4].wait()
    copies[1].wait()

    def await_queries(group):
        first = 1 if group == 0 else 0
        part = qbuf.at[pl.ds(group * y_chips, y_chips - first)]
        pltpu.make_async_remote_copy(
            src_ref=part, dst_ref=part, send_sem=qsend, recv_sem=qrecv.at[group], device_id=(sibling, z), device_id_type=MESH
        ).wait_recv()

    def forward(part):
        begin, count = ((0, 1), (1, x_chips - 1))[part]
        return pltpu.make_async_remote_copy(
            src_ref=qbuf.at[pl.ds(begin * y_chips, count * y_chips)],
            dst_ref=qbuf.at[pl.ds((x_chips + begin) * y_chips, count * y_chips)],
            send_sem=fsend.at[part],
            recv_sem=frecv.at[part],
            device_id=(sibling, z),
            device_id_type=MESH,
        )

    def partials(group):
        return pltpu.make_async_remote_copy(
            src_ref=give.at[group],
            dst_ref=take.at[group],
            send_sem=psend.at[group],
            recv_sem=precv.at[group],
            device_id=(sibling, z),
            device_id_type=MESH,
        )

    def stabiliser(scores_top):
        top = jnp.max(scores_top, axis=1, keepdims=True) * EXP2_SCALE
        return top.astype(BF16).astype(F32)

    def lane_tiles_max(scores):
        tiles = [scores[:, at : at + 128] for at in range(0, scores.shape[1], 128)]
        return functools.reduce(jnp.maximum, tiles)

    def weighted(scores, top, values):
        weights = jnp.exp2(scores * EXP2_SCALE - top).astype(BF16)
        wide = jnp.concatenate([values, jnp.ones(values.shape, BF16)], axis=1)
        return jnp.dot(weights, wide, preferred_element_type=F32)

    def suffix(at):
        holder = sans[at] // 2
        unit = (holder + core) % 2 * x_chips + (holder // (2 * y_chips) - x + x_chips) % x_chips
        rows = qbuf[unit * y_chips + holder // 2 % y_chips]
        scores = lax.dot_general(rows, skb[at], (((1,), (1,)), ((), ())), preferred_element_type=F32)
        position = lax.broadcasted_iota(jnp.int32, scores.shape, 1)
        scores = jnp.where(position < slen[at], scores, NEG_BIG)
        top = stabiliser(lane_tiles_max(scores))
        both = weighted(scores, top, svb[at])
        slot[at, 0] = both[:, :HD]
        slot[at, 1] = both[:, HD:]
        slot[at, 2] = jnp.broadcast_to(top, (ROWS, HD))

    def merged(first, second):
        top = jnp.maximum(first[2], second[2])
        one, two = jnp.exp2(first[2] - top), jnp.exp2(second[2] - top)
        return first[0] * one + second[0] * two, first[1] * one + second[1] * two, top

    def with_slots(part, unit):
        shape = (y_chips, ROWS, HD)
        xx = (x + unit % x_chips) % x_chips
        row = lax.broadcasted_iota(jnp.int32, shape, 1)
        answer = (xx * y_chips + lax.broadcasted_iota(jnp.int32, shape, 0)) * 4 + (core + unit // x_chips) % 2 * 2 + row // PER_GROUP
        part = tuple(value.reshape(shape) for value in part)
        for at in range(2):
            hit = answer == sans[at]
            piece = [jnp.broadcast_to(slot[at, which][None], shape) for which in range(3)]
            part = merged(part, (piece[0], piece[1], jnp.where(hit, piece[2], NEG_BIG)))
        return tuple(value.reshape(unit_rows, HD) for value in part)

    lane = lax.broadcasted_iota(jnp.int32, (unit_rows, HD), 1)

    def send_group(group):
        mine = tuple(own[group, which] for which in range(3))
        mine = with_slots(mine, group)
        stats = take[group, 1]
        theirs = (
            take[group, 0],
            jnp.broadcast_to(stats[:, 64:65], (unit_rows, HD)),
            jnp.broadcast_to(stats[:, 0:1], (unit_rows, HD)),
        )
        total_sum, total, top = merged(mine, theirs)
        high = total.astype(BF16).astype(F32)
        stats = jnp.where(lane < 32, top, jnp.where(lane < 64, high, total - high))
        blocks = pl.ds(group * y_chips, y_chips)
        msg[blocks, 0:ROWS, :] = total_sum.astype(BF16).reshape(y_chips, ROWS, HD)
        msg[blocks, ROWS : 2 * ROWS, :] = stats.astype(BF16).reshape(y_chips, ROWS, HD)

        def send(step):
            yy = (y + step) % y_chips
            pltpu.make_async_remote_copy(
                src_ref=msg.at[group * y_chips + yy],
                dst_ref=got.at[(x_chips - group) % x_chips * y_chips + y],
                send_sem=msend,
                recv_sem=mrecv,
                device_id=(device((x + group) % x_chips, yy), z),
                device_id_type=MESH,
            ).start()

        pl.loop(1, y_chips)(send)

        @pl.when(group != 0)
        def _():
            send(0)

        @pl.when(group == 0)
        def _():
            got[y] = msg[y]

    @pl.loop(0, 2 * x_chips)
    def _(turn):
        unit = turn + 2 * ((turn + 6) // 8) - 6 * ((turn + 2) // 8)

        @pl.when(turn == 0)
        def _():
            await_queries(0)
            forward(0).start()

        @pl.when(turn == 1)
        def _():
            for group in range(1, x_chips):
                await_queries(group)
            forward(1).start()

        @pl.when(turn == 2)
        def _():
            forward(0).wait_recv()
            forward(1).wait_recv()
            copies[2].wait()
            copies[3].wait()
            for at in range(2):
                suffix(at)

        rows = qbuf[pl.ds(unit * y_chips, y_chips)].reshape(unit_rows, HD)
        top = None
        for at in range(0, keys, chunk):
            scores = jnp.dot(rows, kt[:, at : at + chunk], preferred_element_type=F32)
            sbuf[:, at : at + chunk] = scores
            here = lane_tiles_max(scores)
            top = here if top is None else jnp.maximum(top, here)
        top = stabiliser(top)
        both = jnp.zeros((unit_rows, 2 * HD), F32)
        for at in range(0, keys, chunk):
            both += weighted(sbuf[:, at : at + chunk], top, vbuf[at : at + chunk, :])
        part = (both[:, :HD], both[:, HD:], jnp.broadcast_to(top, (unit_rows, HD)))

        @pl.when(unit < x_chips)
        def _():
            for which in range(3):
                own[unit, which] = part[which]

        @pl.when(unit >= x_chips)
        def _():
            total_sum, total, highest = with_slots(part, unit)
            give[unit - x_chips, 0] = total_sum
            give[unit - x_chips, 1] = jnp.where(lane < 64, highest, total)
            partials(unit - x_chips).start()

        @pl.when(turn >= 3)
        def _():
            @pl.when(turn != 5)
            def _():
                group = turn - 3 - turn // 6
                partials(group).wait_recv()
                send_group(group)

    def whole(ref, count, send_sem, recv_sem):
        part = ref.at[pl.ds(0, count)]
        return pltpu.make_async_remote_copy(
            src_ref=part, dst_ref=part, send_sem=send_sem, recv_sem=recv_sem, device_id=(sibling, z), device_id_type=MESH
        )

    whole(got, chips - 1, msend, mrecv).wait_recv()
    sums = got[:, 0:ROWS, :].astype(F32)
    stats = got[:, ROWS : 2 * ROWS, :].astype(F32)
    shape = sums.shape
    tops = jnp.broadcast_to(stats[:, :, 0:1], shape)
    totals = jnp.broadcast_to(stats[:, :, 32:33], shape) + jnp.broadcast_to(stats[:, :, 64:65], shape)
    factor = jnp.exp2(tops - jnp.max(tops, axis=0, keepdims=True))
    result = jnp.sum(sums * factor, axis=0) / jnp.sum(totals * factor, axis=0)
    zbuf[z] = result.astype(BF16)

    @pl.loop(1, z_chips)
    def _(step):
        pltpu.make_async_remote_copy(
            src_ref=zbuf.at[z],
            dst_ref=zbuf.at[z],
            send_sem=zsend,
            recv_sem=zrecv,
            device_id=(seq, (z + step) % z_chips),
            device_id_type=MESH,
        ).start()

    whole(qbuf, chips - 1, qsend, mrecv).wait_send()
    forward(0).wait_send()
    forward(1).wait_send()
    for group in range(x_chips):
        partials(group).wait_send()
    whole(msg, chips - 1, msend, mrecv).wait_send()
    heads = whole(zbuf, z_chips - 1, zsend, zrecv)
    heads.wait_recv()
    out_ref[...] = zbuf[...]
    heads.wait_send()


def on_device(x_chips, queries, prefix_keys, prefix_values, suffix_keys, suffix_values, suffix_length, slot_answer):
    z_chips = lax.axis_size("head")
    chips = lax.axis_size("seq") // 2
    y_chips = chips // x_chips
    keys, cap = prefix_keys.shape[0], suffix_keys.shape[1]
    unit_rows = y_chips * ROWS
    chunk = min(512, keys)
    hbm = pl.BlockSpec(memory_space=pltpu.MemorySpace.HBM)
    vmem = pl.BlockSpec(memory_space=pltpu.VMEM)
    smem = pl.BlockSpec(memory_space=pltpu.SMEM)
    dma = pltpu.SemaphoreType.DMA
    heads = pl.pallas_call(
        functools.partial(attend, x_chips, y_chips, z_chips, chunk),
        out_shape=jax.ShapeDtypeStruct((z_chips, ROWS, HD), BF16),
        in_specs=[vmem, hbm, hbm, hbm, hbm, smem, smem],
        out_specs=vmem,
        scratch_shapes=[
            pltpu.VMEM((2 * chips, ROWS, HD), BF16),
            pltpu.VMEM((keys, HD), BF16),
            pltpu.VMEM((HD, keys), BF16),
            pltpu.VMEM((keys, HD), BF16),
            pltpu.VMEM((2, cap, HD), BF16),
            pltpu.VMEM((2, cap, HD), BF16),
            pltpu.VMEM((unit_rows, keys), F32),
            pltpu.VMEM((x_chips, 3, unit_rows, HD), F32),
            pltpu.VMEM((x_chips, 2, unit_rows, HD), F32),
            pltpu.VMEM((x_chips, 2, unit_rows, HD), F32),
            pltpu.VMEM((2, 3, ROWS, HD), F32),
            pltpu.VMEM((chips, 2 * ROWS, HD), BF16),
            pltpu.VMEM((chips, 2 * ROWS, HD), BF16),
            pltpu.VMEM((z_chips, ROWS, HD), BF16),
            dma((5,)),
            dma,
            dma((x_chips,)),
            dma((2,)),
            dma((2,)),
            dma((x_chips,)),
            dma((x_chips,)),
            dma,
            dma,
            dma,
            dma,
        ],
        compiler_params=pltpu.CompilerParams(collective_id=0, has_side_effects=True, vmem_limit_bytes=48 << 20),
        name="attend",
    )(
        queries.reshape(ROWS, HD),
        prefix_keys,
        prefix_values,
        suffix_keys,
        suffix_values,
        suffix_length,
        slot_answer,
    )
    heads = heads.reshape(z_chips, 2, PER_GROUP * HD)
    return jnp.swapaxes(heads, 0, 1).reshape(2, z_chips * PER_GROUP * HD)


def solution(mesh):
    in_specs = (
        P("seq", "head"),
        P("seq", "head"),
        P("seq", "head"),
        P("seq", None, "head"),
        P("seq", None, "head"),
        P("seq"),
        P("seq"),
    )
    return jax.shard_map(
        functools.partial(on_device, 4), mesh=mesh, in_specs=in_specs, out_specs=P("seq", None), check_vma=False
    )
```

time: 482 us -> 53.8 us (0.11)
  the two profiles are of different devices: /device:TPU:64 before, /device:TPU:6 now
where the time goes in v1:
time: 53.8 us; the launch traced here: 53.5 us
  Pallas kernels  47.2 us (88%)
  local copies, waits for them, and re-layouts  6.25 us (12%)
    pallas_call x1, Pallas kernels, on_device(): pl.pallas_call(functools.partial(attend, x_chips, y_chips, z_chips, chunk...  47.2 us
    unnamed x12, local copies, waits for them, and re-layouts  4.9 us

profile of v1, /device:TPU:6, one launch (start us, length us, event | category | flops | bytes accessed | tf_op | source)
XLA Modules:
  0.0 53.5 jit_solution(14424144339503241611)
XLA Ops:
  0.0 0.0 copy-start.5
  0.0 0.0 copy-start.4
  0.0 0.7 %reshape.9.q_ref = bf16[16,128]{1,0:T(8,128)(2,1)S(1)} reshape(bf16[2,1024]{1,0:T(2,128)(2,1)} %param.7) | data formatting | bytes 8192 | tf_op jit(solution)/shard_map/reshape | solution.py:335
  0.7 0.0 copy-done.5
  0.7 0.0 copy-done.4
  0.7 0.0 copy-start
  0.7 1.2 %copy-done = bf16[4096,128]{1,0:T(8,128)(2,1)S(1)} copy-done((bf16[4096,128]{1,0:T(8,128)(2,1)S(1)}, bf16[4096,128]{1,0:T(8,128)(2,1)}, u32[]{:S(2)}) %copy-start) | copy-done | bytes 1048600
  2.0 0.0 copy-start.1
  2.0 1.2 %copy-done.1 = bf16[4096,128]{1,0:T(8,128)(2,1)S(1)} copy-done((bf16[4096,128]{1,0:T(8,128)(2,1)S(1)}, bf16[4096,128]{1,0:T(8,128)(2,1)}, u32[]{:S(2)}) %copy-start.1) | copy-done | bytes 1048600
  3.2 0.0 copy-start.2
  3.2 1.2 %copy-done.2 = bf16[2,2048,128]{2,1,0:T(8,128)(2,1)S(1)} copy-done((bf16[2,2048,128]{2,1,0:T(8,128)(2,1)S(1)}, bf16[2,2048,128]{2,1,0:T(8,128)(2,1)}, u32[]{:S(2)}) %copy-start.2) | copy-done | bytes 1048600
  4.4 0.0 copy-start.3
  4.4 1.2 %copy-done.3 = bf16[2,2048,128]{2,1,0:T(8,128)(2,1)S(1)} copy-done((bf16[2,2048,128]{2,1,0:T(8,128)(2,1)S(1)}, bf16[2,2048,128]{2,1,0:T(8,128)(2,1)}, u32[]{:S(2)}) %copy-start.3) | copy-done | bytes 1048600
  5.6 47.2 %attend.1 = bf16[8,16,128]{2,1,0:T(8,128)(2,1)S(1)} custom-call(bf16[16,128]{1,0:T(8,128)(2,1)S(1)} %reshape.9.q_ref, bf16[4096,128]{1,0:T(8,128)(2,1)S(1)} %copy-done, bf16[4096,128]{1,0:T(8,128)(2,1)S(1)} %copy-done.1, bf16[2,2048,128]{2,1,0:T(8,128)(2,1)S(1)} %copy-done.2, bf16[2,2048,128]{2,1,0:T(8,128)(2,1)S(1)} %copy-done.3, s32[2]{0:T(128)S(1)} %copy-done.4, ...), custom_call_target="tpu_custom_call" | custom-call | tf_op jit(solution)/shard_map/attend/pallas_call | solution.py:300
  52.9 0.6 %reshape.10 = bf16[8,2,1024]{2,1,0:T(2,128)(2,1)} reshape(bf16[8,16,128]{2,1,0:T(8,128)(2,1)S(1)} %attend.1) | data formatting | bytes 65536 | tf_op jit(solution)/shard_map/reshape | solution.py:343
Async XLA Ops:
  0.0 0.7 %copy-start.5 = (s32[2]{0:T(128)S(1)}, s32[2]{0:T(128)}, u32[]{:S(2)}) copy-start(s32[2]{0:T(128)} %sans.1) | copy-start | bytes 28
  0.0 0.7 %copy-start.4 = (s32[2]{0:T(128)S(1)}, s32[2]{0:T(128)}, u32[]{:S(2)}) copy-start(s32[2]{0:T(128)} %slen.1) | copy-start | bytes 28
  0.7 1.2 %copy-start = (bf16[4096,128]{1,0:T(8,128)(2,1)S(1)}, bf16[4096,128]{1,0:T(8,128)(2,1)}, u32[]{:S(2)}) copy-start(bf16[4096,128]{1,0:T(8,128)(2,1)} %pk.1) | copy-start | bytes 3145732
  2.0 1.2 %copy-start.1 = (bf16[4096,128]{1,0:T(8,128)(2,1)S(1)}, bf16[4096,128]{1,0:T(8,128)(2,1)}, u32[]{:S(2)}) copy-start(bf16[4096,128]{1,0:T(8,128)(2,1)} %pv.1) | copy-start | bytes 3145732
  3.2 1.2 %copy-start.2 = (bf16[2,2048,128]{2,1,0:T(8,128)(2,1)S(1)}, bf16[2,2048,128]{2,1,0:T(8,128)(2,1)}, u32[]{:S(2)}) copy-start(bf16[2,2048,128]{2,1,0:T(8,128)(2,1)} %sk.1) | copy-start | bytes 3145732
  4.4 1.2 %copy-start.3 = (bf16[2,2048,128]{2,1,0:T(8,128)(2,1)S(1)}, bf16[2,2048,128]{2,1,0:T(8,128)(2,1)}, u32[]{:S(2)}) copy-start(bf16[2,2048,128]{2,1,0:T(8,128)(2,1)} %sv.1) | copy-start | bytes 3145732

commit v2 on v1

v2 whole, which is shorter than its diff:
```python
import functools
import math

import jax
import jax.numpy as jnp
from jax import lax
from jax.experimental import pallas as pl
from jax.experimental.pallas import tpu as pltpu
from jax.sharding import PartitionSpec as P

HD = 128
PER_GROUP = 8
NEG_BIG = -1e30
EXP2_SCALE = math.log2(math.e) / math.sqrt(HD)
ROWS = 16
F32 = jnp.float32
BF16 = jnp.bfloat16
MESH = pl.DeviceIdType.MESH


def attend(x_chips, y_chips, z_chips, chunk, q_ref, pk, pv, sk, sv, slen, sans, out_ref, qraw, qown, qbuf, kraw, kt, vbuf, skb, svb,
           even, odd, own, give, take, slot, msg, got, zbuf, local_sem, qsend, qrecv, fsend, frecv, psend, precv, msend, mrecv, zsend, zrecv):
    seq, z = lax.axis_index("seq"), lax.axis_index("head")
    chip = seq // 2
    core = seq - chip * 2
    x = chip // y_chips
    y = chip - x * y_chips
    sibling = chip * 2 + 1 - core
    chips = x_chips * y_chips
    half = chips // 2
    unit_rows = half * ROWS
    keys = kraw.shape[0]

    def start_others(begin, count, me, start):
        @pl.loop(begin, begin + count)
        def _(at):
            @pl.when(at != me)
            def _():
                start(at)

    copies = [
        pltpu.make_async_copy(pk, kraw, local_sem.at[0]),
        pltpu.make_async_copy(pv, vbuf, local_sem.at[1]),
        pltpu.make_async_copy(sk, skb, local_sem.at[2]),
        pltpu.make_async_copy(sv, svb, local_sem.at[3]),
    ]
    query_copy = pltpu.make_async_copy(q_ref, qraw, local_sem.at[4])
    query_copy.start()

    barrier = pltpu.get_barrier_semaphore()

    def greet(to):
        pl.semaphore_signal(barrier, inc=1, device_id=to, device_id_type=MESH)

    start_others(0, chips, chip, lambda at: greet((at * 2 + core, z)))
    greet((sibling, z))
    start_others(0, z_chips, z, lambda at: greet((seq, at)))
    for copy in copies:
        copy.start()

    query_copy.wait()
    raw = qraw[...].astype(F32)
    pieces = [raw[at : at + 1, h * HD : (h + 1) * HD] for at in range(2) for h in range(PER_GROUP)]
    block = jnp.concatenate(pieces, axis=0).astype(BF16)
    qown[...] = block
    qbuf[y] = block
    pl.semaphore_wait(barrier, 1 + (chips - 1) + (z_chips - 1))

    for group in range(x_chips):
        column = (x + x_chips - group) % x_chips * y_chips

        def send_queries(yy, group=group, column=column):
            pltpu.make_async_remote_copy(
                src_ref=qown,
                dst_ref=qbuf.at[group * y_chips + y],
                send_sem=qsend,
                recv_sem=qrecv.at[group],
                device_id=((column + yy) * 2 + core, z),
                device_id_type=MESH,
            ).start()

        if group == 0:
            start_others(0, y_chips, y, send_queries)
        else:
            pl.loop(0, y_chips)(send_queries)

    copies[0].wait()

    @pl.loop(0, keys // chunk)
    def _(step):
        at = pl.multiple_of(step * chunk, chunk)
        kt[:, pl.ds(at, chunk)] = kraw[pl.ds(at, chunk), :].T

    def await_queries(group):
        first = 1 if group == 0 else 0
        part = qbuf.at[pl.ds(group * y_chips, y_chips - first)]
        pltpu.make_async_remote_copy(
            src_ref=part, dst_ref=part, send_sem=qsend, recv_sem=qrecv.at[group], device_id=(sibling, z), device_id_type=MESH
        ).wait_recv()

    def forward(part):
        return pltpu.make_async_remote_copy(
            src_ref=qbuf.at[pl.ds(part * half, half)],
            dst_ref=qbuf.at[pl.ds(chips + part * half, half)],
            send_sem=fsend.at[part],
            recv_sem=frecv.at[part],
            device_id=(sibling, z),
            device_id_type=MESH,
        )

    def partials(part):
        return pltpu.make_async_remote_copy(
            src_ref=give.at[part],
            dst_ref=take.at[part],
            send_sem=psend.at[part],
            recv_sem=precv.at[part],
            device_id=(sibling, z),
            device_id_type=MESH,
        )

    def stabiliser(scores_top):
        top = jnp.max(scores_top, axis=1, keepdims=True) * EXP2_SCALE
        return top.astype(BF16).astype(F32)

    def lane_tiles_max(scores):
        tiles = [scores[:, at : at + 128] for at in range(0, scores.shape[1], 128)]
        return functools.reduce(jnp.maximum, tiles)

    def weighted(scores, top, values):
        weights = jnp.exp2(scores * EXP2_SCALE - top).astype(BF16)
        wide = jnp.concatenate([values, jnp.ones(values.shape, BF16)], axis=1)
        return jnp.dot(weights, wide, preferred_element_type=F32)

    def turn(now, top, begin, later):
        both, later_top = None, None
        rows = None if begin is None else qbuf[begin : begin + half].reshape(unit_rows, HD)
        for at in range(0, keys, chunk):
            if begin is not None:
                scores = jnp.dot(rows, kt[:, at : at + chunk], preferred_element_type=F32)
                later[:, at : at + chunk] = scores
                here = lane_tiles_max(scores)
                later_top = here if later_top is None else jnp.maximum(later_top, here)
            if now is not None:
                here = weighted(now[:, at : at + chunk], top, vbuf[at : at + chunk, :])
                both = here if both is None else both + here
        part = None if now is None else (both[:, :HD], both[:, HD:], jnp.broadcast_to(top, (unit_rows, HD)))
        return part, None if begin is None else stabiliser(later_top)

    def suffix(at):
        holder = sans[at] // 2
        block = (holder + core) % 2 * chips + (holder // 2 - x * y_chips + chips) % chips
        scores = lax.dot_general(qbuf[block], skb[at], (((1,), (1,)), ((), ())), preferred_element_type=F32)
        position = lax.broadcasted_iota(jnp.int32, scores.shape, 1)
        scores = jnp.where(position < slen[at], scores, NEG_BIG)
        top = stabiliser(lane_tiles_max(scores))
        both = weighted(scores, top, svb[at])
        slot[at, 0] = both[:, :HD]
        slot[at, 1] = both[:, HD:]
        slot[at, 2] = jnp.broadcast_to(top, (ROWS, HD))

    def merged(first, second):
        top = jnp.maximum(first[2], second[2])
        one, two = jnp.exp2(first[2] - top), jnp.exp2(second[2] - top)
        return first[0] * one + second[0] * two, first[1] * one + second[1] * two, top

    shape = (half, ROWS, HD)
    place = lax.broadcasted_iota(jnp.int32, shape, 0)
    second_row = jnp.where(lax.broadcasted_iota(jnp.int32, shape, 1) < PER_GROUP, 0, 1)

    def with_slots(value, part, mine):
        at = place + x * y_chips + part * half
        at = jnp.where(at < chips, at, at - chips)
        answer = at * 4 + second_row + 2 * (core if mine else 1 - core)
        value = tuple(each.reshape(shape) for each in value)
        hits = [answer == sans[at] for at in range(2)]
        held = [[jnp.broadcast_to(slot[at, which][None], shape) for which in range(3)] for at in range(2)]
        piece = [jnp.where(hits[0], held[0][which], held[1][which]) for which in range(3)]
        piece[2] = jnp.where(hits[0], held[0][2], jnp.where(hits[1], held[1][2], NEG_BIG))
        return tuple(each.reshape(unit_rows, HD) for each in merged(value, piece))

    lane = lax.broadcasted_iota(jnp.int32, (unit_rows, HD), 1)

    def give_half(part, value):
        total_sum, total, top = with_slots(value, part, False)
        give[part, 0] = total_sum
        give[part, 1] = jnp.where(lane < 64, top, total)
        partials(part).start()

    def send_half(part, mine):
        mine = with_slots(mine, part, True)
        partials(part).wait_recv()
        stats = take[part, 1]
        theirs = (
            take[part, 0],
            jnp.broadcast_to(stats[:, 64:65], (unit_rows, HD)),
            jnp.broadcast_to(stats[:, 0:1], (unit_rows, HD)),
        )
        total_sum, total, top = merged(mine, theirs)
        high = total.astype(BF16).astype(F32)
        stats = jnp.where(lane < 32, top, jnp.where(lane < 64, high, total - high))
        blocks = pl.ds(part * half, half)
        msg[blocks, 0:ROWS, :] = total_sum.astype(BF16).reshape(shape)
        msg[blocks, ROWS : 2 * ROWS, :] = stats.astype(BF16).reshape(shape)
        for group in range(part * x_chips // 2, (part + 1) * x_chips // 2):
            column = (x + group) % x_chips * y_chips

            def send(yy, group=group, column=column):
                pltpu.make_async_remote_copy(
                    src_ref=msg.at[group * y_chips + yy],
                    dst_ref=got.at[(x_chips - group) % x_chips * y_chips + y],
                    send_sem=msend,
                    recv_sem=mrecv,
                    device_id=((column + yy) * 2 + core, z),
                    device_id_type=MESH,
                ).start()

            if group == 0:
                start_others(0, y_chips, y, send)
                got[y] = msg[y]
            else:
                pl.loop(0, y_chips)(send)

    for group in range(x_chips // 2):
        await_queries(group)
    forward(0).start()
    _, top = turn(None, None, 0, even)
    for group in range(x_chips // 2, x_chips):
        await_queries(group)
    forward(1).start()
    copies[1].wait()
    forward(0).wait_recv()
    own_first, top = turn(even, top, chips, odd)
    for which in range(3):
        own[which] = own_first[which]
    forward(1).wait_recv()
    copies[2].wait()
    copies[3].wait()
    for at in range(2):
        suffix(at)
    other, top = turn(odd, top, chips + half, even)
    give_half(0, other)
    other, top = turn(even, top, half, odd)
    give_half(1, other)
    send_half(0, tuple(own[which] for which in range(3)))
    own_second, _ = turn(odd, top, None, None)
    send_half(1, own_second)

    def whole(ref, count, send_sem, recv_sem):
        part = ref.at[pl.ds(0, count)]
        return pltpu.make_async_remote_copy(
            src_ref=part, dst_ref=part, send_sem=send_sem, recv_sem=recv_sem, device_id=(sibling, z), device_id_type=MESH
        )

    whole(got, chips - 1, msend, mrecv).wait_recv()
    sums = got[:, 0:ROWS, :].astype(F32)
    stats = got[:, ROWS : 2 * ROWS, :].astype(F32)
    tops = jnp.broadcast_to(stats[:, :, 0:1], sums.shape)
    totals = jnp.broadcast_to(stats[:, :, 32:33], sums.shape) + jnp.broadcast_to(stats[:, :, 64:65], sums.shape)
    factor = jnp.exp2(tops - jnp.max(tops, axis=0, keepdims=True))
    result = jnp.sum(sums * factor, axis=0) / jnp.sum(totals * factor, axis=0)
    zbuf[z] = result.astype(BF16)

    def send_result(to):
        pltpu.make_async_remote_copy(
            src_ref=zbuf.at[z], dst_ref=zbuf.at[z], send_sem=zsend, recv_sem=zrecv, device_id=(seq, to), device_id_type=MESH
        ).start()

    start_others(0, z_chips, z, send_result)

    whole(qbuf, chips - 1, qsend, mrecv).wait_send()
    for part in range(2):
        forward(part).wait_send()
        partials(part).wait_send()
    whole(msg, chips - 1, msend, mrecv).wait_send()
    heads = whole(zbuf, z_chips - 1, zsend, zrecv)
    heads.wait_recv()
    out_ref[...] = zbuf[...]
    heads.wait_send()


def on_device(x_chips, queries, prefix_keys, prefix_values, suffix_keys, suffix_values, suffix_length, slot_answer):
    z_chips = lax.axis_size("head")
    chips = lax.axis_size("seq") // 2
    y_chips = chips // x_chips
    keys, cap = prefix_keys.shape[0], suffix_keys.shape[1]
    unit_rows = chips // 2 * ROWS
    chunk = min(1024, keys)
    hbm = pl.BlockSpec(memory_space=pltpu.MemorySpace.HBM)
    vmem = pl.BlockSpec(memory_space=pltpu.VMEM)
    smem = pl.BlockSpec(memory_space=pltpu.SMEM)
    dma = pltpu.SemaphoreType.DMA
    heads = pl.pallas_call(
        functools.partial(attend, x_chips, y_chips, z_chips, chunk),
        out_shape=jax.ShapeDtypeStruct((z_chips, ROWS, HD), BF16),
        in_specs=[hbm, hbm, hbm, hbm, hbm, smem, smem],
        out_specs=vmem,
        scratch_shapes=[
            pltpu.VMEM((2, PER_GROUP * HD), BF16),
            pltpu.VMEM((ROWS, HD), BF16),
            pltpu.VMEM((2 * chips, ROWS, HD), BF16),
            pltpu.VMEM((keys, HD), BF16),
            pltpu.VMEM((HD, keys), BF16),
            pltpu.VMEM((keys, HD), BF16),
            pltpu.VMEM((2, cap, HD), BF16),
            pltpu.VMEM((2, cap, HD), BF16),
            pltpu.VMEM((unit_rows, keys), F32),
            pltpu.VMEM((unit_rows, keys), F32),
            pltpu.VMEM((3, unit_rows, HD), F32),
            pltpu.VMEM((2, 2, unit_rows, HD), F32),
            pltpu.VMEM((2, 2, unit_rows, HD), F32),
            pltpu.VMEM((2, 3, ROWS, HD), F32),
            pltpu.VMEM((chips, 2 * ROWS, HD), BF16),
            pltpu.VMEM((chips, 2 * ROWS, HD), BF16),
            pltpu.VMEM((z_chips, ROWS, HD), BF16),
            dma((5,)),
            dma,
            dma((x_chips,)),
            dma((2,)),
            dma((2,)),
            dma((2,)),
            dma((2,)),
            dma,
            dma,
            dma,
            dma,
        ],
        compiler_params=pltpu.CompilerParams(collective_id=0, has_side_effects=True, vmem_limit_bytes=60 << 20),
        name="attend",
    )(
        queries,
        prefix_keys,
        prefix_values,
        suffix_keys,
        suffix_values,
        suffix_length,
        slot_answer,
    )
    heads = heads.reshape(z_chips, 2, PER_GROUP * HD)
    return jnp.swapaxes(heads, 0, 1).reshape(2, z_chips * PER_GROUP * HD)


def solution(mesh):
    in_specs = (
        P("seq", "head"),
        P("seq", "head"),
        P("seq", "head"),
        P("seq", None, "head"),
        P("seq", None, "head"),
        P("seq"),
        P("seq"),
    )
    return jax.shard_map(
        functools.partial(on_device, 4), mesh=mesh, in_specs=in_specs, out_specs=P("seq", None), check_vma=False
    )
```

time: 53.8 us -> 45.1 us (0.84)
  local copies, waits for them, and re-layouts: 6.25 us -> 1.39 us
  Pallas kernels: 47.2 us -> 43.5 us
    unnamed x12 -> x0, local copies, waits for them, and re-layouts: 4.9 us -> none
    pallas_call x1, Pallas kernels: 47.2 us -> 43.5 us  [on_device(): pl.pallas_call(functools.partial(attend, x_chips, y_chips, z_chips, chunk...]
    reshape x1, local copies, waits for them, and re-layouts: 0.63 us -> 1.39 us  [on_device(): heads = heads.reshape(z_chips, 2, PER_GROUP * HD)]
    reshape x1 -> x0, local copies, waits for them, and re-layouts: 0.72 us -> none  [on_device(): queries.reshape(ROWS, HD)]
where the time goes in v2:
time: 45.1 us; the launch traced here: 44.9 us
  Pallas kernels  43.5 us (96%)
  local copies, waits for them, and re-layouts  1.39 us (3%)
    pallas_call x1, Pallas kernels, on_device(): pl.pallas_call(functools.partial(attend, x_chips, y_chips, z_chips, chunk...  43.5 us
    reshape x1, local copies, waits for them, and re-layouts, on_device(): heads = heads.reshape(z_chips, 2, PER_GROUP * HD)  1.39 us

profile of v2, /device:TPU:6, one launch (start us, length us, event | category | flops | bytes accessed | tf_op | source)
XLA Modules:
  0.0 44.9 jit_solution(1055233249099633910)
XLA Ops:
  0.0 43.5 %attend.1 = bf16[8,16,128]{2,1,0:T(8,128)(2,1)} custom-call(bf16[2,1024]{1,0:T(2,128)(2,1)} %q_ref.1, bf16[4096,128]{1,0:T(8,128)(2,1)} %pk.1, bf16[4096,128]{1,0:T(8,128)(2,1)} %pv.1, bf16[2,2048,128]{2,1,0:T(8,128)(2,1)} %sk.1, bf16[2,2048,128]{2,1,0:T(8,128)(2,1)} %sv.1, s32[2]{0:T(128)} %slen.1, s32[2]{0:T(128)} %sans.1), custom_call_target="tpu_custom_call" | custom-call | tf_op jit(solution)/shard_map/attend/pallas_call | solution.py:292
  43.5 1.4 %reshape.6 = bf16[8,2,1024]{2,1,0:T(2,128)(2,1)} reshape(bf16[8,16,128]{2,1,0:T(8,128)(2,1)} %attend.1) | data formatting | bytes 65536 | tf_op jit(solution)/shard_map/reshape | solution.py:338

commit v3 on v2

--- a/solution.py
+++ b/solution.py
@@ -31,12 +31,9 @@
     unit_rows = half * ROWS
     keys = kraw.shape[0]
 
-    def start_others(begin, count, me, start):
-        @pl.loop(begin, begin + count)
-        def _(at):
-            @pl.when(at != me)
-            def _():
-                start(at)
+    def others(count, me, act):
+        for step in range(1, count):
+            act(lax.rem(me + step, count))
 
     copies = [
         pltpu.make_async_copy(pk, kraw, local_sem.at[0]),
@@ -52,9 +49,13 @@
     def greet(to):
         pl.semaphore_signal(barrier, inc=1, device_id=to, device_id_type=MESH)
 
-    start_others(0, chips, chip, lambda at: greet((at * 2 + core, z)))
+    columns = [lax.rem(x + group, x_chips) * y_chips for group in range(x_chips)]
+    others(z_chips, z, lambda at: greet((seq, at)))
+    for group in range(1, x_chips):
+        for yy in range(y_chips):
+            greet(((columns[group] + yy) * 2 + core, z))
+    others(y_chips, y, lambda at: greet(((columns[0] + at) * 2 + core, z)))
     greet((sibling, z))
-    start_others(0, z_chips, z, lambda at: greet((seq, at)))
     for copy in copies:
         copy.start()
 
@@ -67,7 +68,7 @@
     pl.semaphore_wait(barrier, 1 + (chips - 1) + (z_chips - 1))
 
     for group in range(x_chips):
-        column = (x + x_chips - group) % x_chips * y_chips
+        column = columns[(x_chips - group) % x_chips]
 
         def send_queries(yy, group=group, column=column):
             pltpu.make_async_remote_copy(
@@ -80,9 +81,10 @@
             ).start()
 
         if group == 0:
-            start_others(0, y_chips, y, send_queries)
+            others(y_chips, y, send_queries)
         else:
-            pl.loop(0, y_chips)(send_queries)
+            for yy in range(y_chips):
+                send_queries(yy)
 
     copies[0].wait()
 
@@ -131,10 +133,12 @@
         wide = jnp.concatenate([values, jnp.ones(values.shape, BF16)], axis=1)
         return jnp.dot(weights, wide, preferred_element_type=F32)
 
-    def turn(now, top, begin, later):
+    def turn(now, top, begin, later, midway=None):
         both, later_top = None, None
         rows = None if begin is None else qbuf[begin : begin + half].reshape(unit_rows, HD)
         for at in range(0, keys, chunk):
+            if midway is not None and at == keys // 2:
+                midway()
             if begin is not None:
                 scores = jnp.dot(rows, kt[:, at : at + chunk], preferred_element_type=F32)
                 later[:, at : at + chunk] = scores
@@ -202,7 +206,7 @@
         msg[blocks, 0:ROWS, :] = total_sum.astype(BF16).reshape(shape)
         msg[blocks, ROWS : 2 * ROWS, :] = stats.astype(BF16).reshape(shape)
         for group in range(part * x_chips // 2, (part + 1) * x_chips // 2):
-            column = (x + group) % x_chips * y_chips
+            column = columns[group]
 
             def send(yy, group=group, column=column):
                 pltpu.make_async_remote_copy(
@@ -215,10 +219,11 @@
                 ).start()
 
             if group == 0:
-                start_others(0, y_chips, y, send)
+                others(y_chips, y, send)
                 got[y] = msg[y]
             else:
-                pl.loop(0, y_chips)(send)
+                for yy in range(y_chips):
+                    send(yy)
 
     for group in range(x_chips // 2):
         await_queries(group)
@@ -239,9 +244,8 @@
         suffix(at)
     other, top = turn(odd, top, chips + half, even)
     give_half(0, other)
-    other, top = turn(even, top, half, odd)
+    other, top = turn(even, top, half, odd, lambda: send_half(0, tuple(own[which] for which in range(3))))
     give_half(1, other)
-    send_half(0, tuple(own[which] for which in range(3)))
     own_second, _ = turn(odd, top, None, None)
     send_half(1, own_second)
 
@@ -258,14 +262,15 @@
     totals = jnp.broadcast_to(stats[:, :, 32:33], sums.shape) + jnp.broadcast_to(stats[:, :, 64:65], sums.shape)
     factor = jnp.exp2(tops - jnp.max(tops, axis=0, keepdims=True))
     result = jnp.sum(sums * factor, axis=0) / jnp.sum(totals * factor, axis=0)
-    zbuf[z] = result.astype(BF16)
+    wide = [jnp.concatenate([result[at * PER_GROUP + h][None] for h in range(PER_GROUP)], axis=1) for at in range(2)]
+    zbuf[z] = jnp.concatenate(wide, axis=0).astype(BF16)
 
     def send_result(to):
         pltpu.make_async_remote_copy(
             src_ref=zbuf.at[z], dst_ref=zbuf.at[z], send_sem=zsend, recv_sem=zrecv, device_id=(seq, to), device_id_type=MESH
         ).start()
 
-    start_others(0, z_chips, z, send_result)
+    others(z_chips, z, send_result)
 
     whole(qbuf, chips - 1, qsend, mrecv).wait_send()
     for part in range(2):
@@ -291,7 +296,7 @@
     dma = pltpu.SemaphoreType.DMA
     heads = pl.pallas_call(
         functools.partial(attend, x_chips, y_chips, z_chips, chunk),
-        out_shape=jax.ShapeDtypeStruct((z_chips, ROWS, HD), BF16),
+        out_shape=jax.ShapeDtypeStruct((z_chips, 2, PER_GROUP * HD), BF16),
         in_specs=[hbm, hbm, hbm, hbm, hbm, smem, smem],
         out_specs=vmem,
         scratch_shapes=[
@@ -311,7 +316,7 @@
             pltpu.VMEM((2, 3, ROWS, HD), F32),
             pltpu.VMEM((chips, 2 * ROWS, HD), BF16),
             pltpu.VMEM((chips, 2 * ROWS, HD), BF16),
-            pltpu.VMEM((z_chips, ROWS, HD), BF16),
+            pltpu.VMEM((z_chips, 2, PER_GROUP * HD), BF16),
             dma((5,)),
             dma,
             dma((x_chips,)),
@@ -335,7 +340,6 @@
         suffix_length,
         slot_answer,
     )
-    heads = heads.reshape(z_chips, 2, PER_GROUP * HD)
     return jnp.swapaxes(heads, 0, 1).reshape(2, z_chips * PER_GROUP * HD)
 
 

time: 45.1 us -> 44.4 us (0.984)
  Pallas kernels: 43.5 us -> 42.7 us
    unnamed x0 -> x1, local copies, waits for them, and re-layouts: none -> 1.4 us
    reshape x1 -> x0, local copies, waits for them, and re-layouts: 1.39 us -> none  [on_device(): heads = heads.reshape(z_chips, 2, PER_GROUP * HD)]
    pallas_call x1, Pallas kernels: 43.5 us -> 42.7 us  [on_device(): pl.pallas_call(functools.partial(attend, x_chips, y_chips, z_chips, chunk...]
where the time goes in v3:
time: 44.4 us; the launch traced here: 44.1 us
  Pallas kernels  42.7 us (96%)
  local copies, waits for them, and re-layouts  1.4 us (3%)
    pallas_call x1, Pallas kernels, on_device(): pl.pallas_call(functools.partial(attend, x_chips, y_chips, z_chips, chunk...  42.7 us
    unnamed x1, local copies, waits for them, and re-layouts  1.4 us

profile of v3, /device:TPU:6, one launch (start us, length us, event | category | flops | bytes accessed | tf_op | source)
XLA Modules:
  0.0 44.1 jit_solution(12863955687395556099)
XLA Ops:
  0.0 42.7 %attend.1 = bf16[8,2,1024]{2,1,0:T(2,128)(2,1)} custom-call(bf16[2,1024]{1,0:T(2,128)(2,1)} %q_ref.1, bf16[4096,128]{1,0:T(8,128)(2,1)} %pk.1, bf16[4096,128]{1,0:T(8,128)(2,1)} %pv.1, bf16[2,2048,128]{2,1,0:T(8,128)(2,1)} %sk.1, bf16[2,2048,128]{2,1,0:T(8,128)(2,1)} %sv.1, s32[2]{0:T(128)} %slen.1, s32[2]{0:T(128)} %sans.1), custom_call_target="tpu_custom_call" | custom-call | tf_op jit(solution)/shard_map/attend/pallas_call | solution.py:297
  42.7 1.4 %copy.9 = bf16[2,8192]{1,0:T(2,128)(2,1)} copy(bf16[2,8192]{1,0:T(2,128)(2,1)} %bitcast.3) | data formatting | bytes 65536

commit v4 on v3

--- a/solution.py
+++ b/solution.py
@@ -18,7 +18,7 @@
 MESH = pl.DeviceIdType.MESH
 
 
-def attend(x_chips, y_chips, z_chips, chunk, q_ref, pk, pv, sk, sv, slen, sans, out_ref, qraw, qown, qbuf, kraw, kt, vbuf, skb, svb,
+def attend(x_chips, y_chips, z_chips, chunk, q_ref, pk, pv, sk, sv, slen, sans, out_ref, qraw, qown, qbuf, keys_here, vbuf, skb, svb,
            even, odd, own, give, take, slot, msg, got, zbuf, local_sem, qsend, qrecv, fsend, frecv, psend, precv, msend, mrecv, zsend, zrecv):
     seq, z = lax.axis_index("seq"), lax.axis_index("head")
     chip = seq // 2
@@ -29,14 +29,14 @@
     chips = x_chips * y_chips
     half = chips // 2
     unit_rows = half * ROWS
-    keys = kraw.shape[0]
+    keys = keys_here.shape[0]
 
     def others(count, me, act):
         for step in range(1, count):
             act(lax.rem(me + step, count))
 
     copies = [
-        pltpu.make_async_copy(pk, kraw, local_sem.at[0]),
+        pltpu.make_async_copy(pk, keys_here, local_sem.at[0]),
         pltpu.make_async_copy(pv, vbuf, local_sem.at[1]),
         pltpu.make_async_copy(sk, skb, local_sem.at[2]),
         pltpu.make_async_copy(sv, svb, local_sem.at[3]),
@@ -88,11 +88,6 @@
 
     copies[0].wait()
 
-    @pl.loop(0, keys // chunk)
-    def _(step):
-        at = pl.multiple_of(step * chunk, chunk)
-        kt[:, pl.ds(at, chunk)] = kraw[pl.ds(at, chunk), :].T
-
     def await_queries(group):
         first = 1 if group == 0 else 0
         part = qbuf.at[pl.ds(group * y_chips, y_chips - first)]
@@ -133,6 +128,9 @@
         wide = jnp.concatenate([values, jnp.ones(values.shape, BF16)], axis=1)
         return jnp.dot(weights, wide, preferred_element_type=F32)
 
+    def inner(rows, columns):
+        return lax.dot_general(rows, columns, (((1,), (1,)), ((), ())), preferred_element_type=F32)
+
     def turn(now, top, begin, later, midway=None):
         both, later_top = None, None
         rows = None if begin is None else qbuf[begin : begin + half].reshape(unit_rows, HD)
@@ -140,7 +138,7 @@
             if midway is not None and at == keys // 2:
                 midway()
             if begin is not None:
-                scores = jnp.dot(rows, kt[:, at : at + chunk], preferred_element_type=F32)
+                scores = inner(rows, keys_here[at : at + chunk, :])
                 later[:, at : at + chunk] = scores
                 here = lane_tiles_max(scores)
                 later_top = here if later_top is None else jnp.maximum(later_top, here)
@@ -153,7 +151,7 @@
     def suffix(at):
         holder = sans[at] // 2
         block = (holder + core) % 2 * chips + (holder // 2 - x * y_chips + chips) % chips
-        scores = lax.dot_general(qbuf[block], skb[at], (((1,), (1,)), ((), ())), preferred_element_type=F32)
+        scores = inner(qbuf[block], skb[at])
         position = lax.broadcasted_iota(jnp.int32, scores.shape, 1)
         scores = jnp.where(position < slen[at], scores, NEG_BIG)
         top = stabiliser(lane_tiles_max(scores))
@@ -283,7 +281,8 @@
     heads.wait_send()
 
 
-def on_device(x_chips, queries, prefix_keys, prefix_values, suffix_keys, suffix_values, suffix_length, slot_answer):
+def on_device(x_chips, *arrays):
+    _, prefix_keys, _, suffix_keys, _, _, _ = arrays
     z_chips = lax.axis_size("head")
     chips = lax.axis_size("seq") // 2
     y_chips = chips // x_chips
@@ -296,7 +295,7 @@
     dma = pltpu.SemaphoreType.DMA
     heads = pl.pallas_call(
         functools.partial(attend, x_chips, y_chips, z_chips, chunk),
-        out_shape=jax.ShapeDtypeStruct((z_chips, 2, PER_GROUP * HD), BF16),
+        out_shape=pltpu.VMEM((z_chips, 2, PER_GROUP * HD), BF16),
         in_specs=[hbm, hbm, hbm, hbm, hbm, smem, smem],
         out_specs=vmem,
         scratch_shapes=[
@@ -304,7 +303,6 @@
             pltpu.VMEM((ROWS, HD), BF16),
             pltpu.VMEM((2 * chips, ROWS, HD), BF16),
             pltpu.VMEM((keys, HD), BF16),
-            pltpu.VMEM((HD, keys), BF16),
             pltpu.VMEM((keys, HD), BF16),
             pltpu.VMEM((2, cap, HD), BF16),
             pltpu.VMEM((2, cap, HD), BF16),
@@ -329,16 +327,10 @@
             dma,
             dma,
         ],
-        compiler_params=pltpu.CompilerParams(collective_id=0, has_side_effects=True, vmem_limit_bytes=60 << 20),
+        compiler_params=pltpu.CompilerParams(collective_id=0, has_side_effects=True, vmem_limit_bytes=56 << 20),
         name="attend",
     )(
-        queries,
-        prefix_keys,
-        prefix_values,
-        suffix_keys,
-        suffix_values,
-        suffix_length,
-        slot_answer,
+        *(pltpu.with_memory_space_constraint(each, pltpu.MemorySpace.HBM) for each in arrays)
     )
     return jnp.swapaxes(heads, 0, 1).reshape(2, z_chips * PER_GROUP * HD)
 

time: 44.4 us -> 43 us (0.968)
  local copies, waits for them, and re-layouts: 1.4 us -> 0.62 us
  Pallas kernels: 42.7 us -> 42.1 us
    unnamed x1, local copies, waits for them, and re-layouts: 1.4 us -> 0.62 us
    pallas_call x1, Pallas kernels: 42.7 us -> 42.1 us  [on_device(): pl.pallas_call(functools.partial(attend, x_chips, y_chips, z_chips, chunk...]
where the time goes in v4:
time: 43 us; the launch traced here: 42.7 us
  Pallas kernels  42.1 us (98%)
  local copies, waits for them, and re-layouts  0.62 us (1%)
    pallas_call x1, Pallas kernels, on_device(): pl.pallas_call(functools.partial(attend, x_chips, y_chips, z_chips, chunk...  42.1 us

profile of v4, /device:TPU:6, one launch (start us, length us, event | category | flops | bytes accessed | tf_op | source)
XLA Modules:
  0.0 42.7 jit_solution(16761673265659707111)
XLA Ops:
  0.0 42.1 %attend.1 = bf16[8,2,1024]{2,1,0:T(2,128)(2,1)S(1)} custom-call(bf16[2,1024]{1,0:T(2,128)(2,1)} %q_ref.1, bf16[4096,128]{1,0:T(8,128)(2,1)} %pk.1, bf16[4096,128]{1,0:T(8,128)(2,1)} %pv.1, bf16[2,2048,128]{2,1,0:T(8,128)(2,1)} %sk.1, bf16[2,2048,128]{2,1,0:T(8,128)(2,1)} %sv.1, s32[2]{0:T(128)} %slen.1, s32[2]{0:T(128)} %sans.1), custom_call_target="tpu_custom_call" | custom-call | tf_op jit(solution)/shard_map/attend/pallas_call | solution.py:296
  42.1 0.6 %copy.9 = bf16[2,8192]{1,0:T(2,128)(2,1)} copy(bf16[2,8192]{1,0:T(2,128)(2,1)S(1)} %bitcast.3) | data formatting | bytes 65536

commit v5 on v4

--- a/solution.py
+++ b/solution.py
@@ -19,7 +19,8 @@
 
 
 def attend(x_chips, y_chips, z_chips, chunk, q_ref, pk, pv, sk, sv, slen, sans, out_ref, qraw, qown, qbuf, keys_here, vbuf, skb, svb,
-           even, odd, own, give, take, slot, msg, got, zbuf, local_sem, qsend, qrecv, fsend, frecv, psend, precv, msend, mrecv, zsend, zrecv):
+           even, odd, own, give, take, slot, msg, got, stat, gotstat, zbuf, local_sem, qsend, qrecv, fsend, frecv, psend, precv, msend, mrecv,
+           ssend, srecv, zsend, zrecv):
     seq, z = lax.axis_index("seq"), lax.axis_index("head")
     chip = seq // 2
     core = seq - chip * 2
@@ -95,12 +96,12 @@
             src_ref=part, dst_ref=part, send_sem=qsend, recv_sem=qrecv.at[group], device_id=(sibling, z), device_id_type=MESH
         ).wait_recv()
 
-    def forward(part):
+    def forward(group):
         return pltpu.make_async_remote_copy(
-            src_ref=qbuf.at[pl.ds(part * half, half)],
-            dst_ref=qbuf.at[pl.ds(chips + part * half, half)],
-            send_sem=fsend.at[part],
-            recv_sem=frecv.at[part],
+            src_ref=qbuf.at[pl.ds(group * y_chips, y_chips)],
+            dst_ref=qbuf.at[pl.ds(chips + group * y_chips, y_chips)],
+            send_sem=fsend.at[group],
+            recv_sem=frecv.at[group],
             device_id=(sibling, z),
             device_id_type=MESH,
         )
@@ -131,21 +132,23 @@
     def inner(rows, columns):
         return lax.dot_general(rows, columns, (((1,), (1,)), ((), ())), preferred_element_type=F32)
 
-    def turn(now, top, begin, later, midway=None):
+    def turn(now, top, begin, later, midway=None, piece=None):
         both, later_top = None, None
-        rows = None if begin is None else qbuf[begin : begin + half].reshape(unit_rows, HD)
+        span = slice(0, unit_rows) if piece is None else piece
+        size = span.stop - span.start
+        rows = None if begin is None else qbuf[begin : begin + size // ROWS].reshape(size, HD)
         for at in range(0, keys, chunk):
             if midway is not None and at == keys // 2:
                 midway()
             if begin is not None:
                 scores = inner(rows, keys_here[at : at + chunk, :])
-                later[:, at : at + chunk] = scores
+                later[span, at : at + chunk] = scores
                 here = lane_tiles_max(scores)
                 later_top = here if later_top is None else jnp.maximum(later_top, here)
             if now is not None:
-                here = weighted(now[:, at : at + chunk], top, vbuf[at : at + chunk, :])
+                here = weighted(now[span, at : at + chunk], top, vbuf[at : at + chunk, :])
                 both = here if both is None else both + here
-        part = None if now is None else (both[:, :HD], both[:, HD:], jnp.broadcast_to(top, (unit_rows, HD)))
+        part = None if now is None else (both[:, :HD], both[:, HD:], jnp.broadcast_to(top, (size, HD)))
         return part, None if begin is None else stabiliser(later_top)
 
     def suffix(at):
@@ -165,12 +168,12 @@
         one, two = jnp.exp2(first[2] - top), jnp.exp2(second[2] - top)
         return first[0] * one + second[0] * two, first[1] * one + second[1] * two, top
 
-    shape = (half, ROWS, HD)
-    place = lax.broadcasted_iota(jnp.int32, shape, 0)
-    second_row = jnp.where(lax.broadcasted_iota(jnp.int32, shape, 1) < PER_GROUP, 0, 1)
-
-    def with_slots(value, part, mine):
-        at = place + x * y_chips + part * half
+    def with_slots(value, first, mine):
+        size = value[0].shape[0]
+        shape = (size // ROWS, ROWS, HD)
+        place = lax.broadcasted_iota(jnp.int32, shape, 0)
+        second_row = jnp.where(lax.broadcasted_iota(jnp.int32, shape, 1) < PER_GROUP, 0, 1)
+        at = place + (x * y_chips + first)
         at = jnp.where(at < chips, at, at - chips)
         answer = at * 4 + second_row + 2 * (core if mine else 1 - core)
         value = tuple(each.reshape(shape) for each in value)
@@ -178,74 +181,94 @@
         held = [[jnp.broadcast_to(slot[at, which][None], shape) for which in range(3)] for at in range(2)]
         piece = [jnp.where(hits[0], held[0][which], held[1][which]) for which in range(3)]
         piece[2] = jnp.where(hits[0], held[0][2], jnp.where(hits[1], held[1][2], NEG_BIG))
-        return tuple(each.reshape(unit_rows, HD) for each in merged(value, piece))
-
-    lane = lax.broadcasted_iota(jnp.int32, (unit_rows, HD), 1)
+        return tuple(each.reshape(size, HD) for each in merged(value, piece))
 
     def give_half(part, value):
-        total_sum, total, top = with_slots(value, part, False)
+        total_sum, total, top = with_slots(value, part * half, False)
+        lane = lax.broadcasted_iota(jnp.int32, total.shape, 1)
         give[part, 0] = total_sum
         give[part, 1] = jnp.where(lane < 64, top, total)
         partials(part).start()
 
-    def send_half(part, mine):
-        mine = with_slots(mine, part, True)
-        partials(part).wait_recv()
-        stats = take[part, 1]
+    def diagonal(shape, begin):
+        return lax.broadcasted_iota(jnp.int32, shape, 2) == lax.broadcasted_iota(jnp.int32, shape, 1) + begin
+
+    def send_groups(groups, mine):
+        first, size = groups[0] * y_chips, len(groups) * y_chips * ROWS
+        part = first // half
+        mine = with_slots(mine, first, True)
+        span = slice((first - part * half) * ROWS, (first - part * half) * ROWS + size)
+        stats = take[part, 1, span]
         theirs = (
-            take[part, 0],
-            jnp.broadcast_to(stats[:, 64:65], (unit_rows, HD)),
-            jnp.broadcast_to(stats[:, 0:1], (unit_rows, HD)),
-        )
-        total_sum, total, top = merged(mine, theirs)
-        high = total.astype(BF16).astype(F32)
-        stats = jnp.where(lane < 32, top, jnp.where(lane < 64, high, total - high))
-        blocks = pl.ds(part * half, half)
-        msg[blocks, 0:ROWS, :] = total_sum.astype(BF16).reshape(shape)
-        msg[blocks, ROWS : 2 * ROWS, :] = stats.astype(BF16).reshape(shape)
-        for group in range(part * x_chips // 2, (part + 1) * x_chips // 2):
-            column = columns[group]
-
-            def send(yy, group=group, column=column):
-                pltpu.make_async_remote_copy(
-                    src_ref=msg.at[group * y_chips + yy],
-                    dst_ref=got.at[(x_chips - group) % x_chips * y_chips + y],
-                    send_sem=msend,
-                    recv_sem=mrecv,
-                    device_id=((column + yy) * 2 + core, z),
-                    device_id_type=MESH,
-                ).start()
+            take[part, 0, span],
+            jnp.broadcast_to(stats[:, 64:65], (size, HD)),
+            jnp.broadcast_to(stats[:, 0:1], (size, HD)),
+        )
+        shape = (size // ROWS, ROWS, HD)
+        total_sum, total, top = (each.reshape(shape) for each in merged(mine, theirs))
+        blocks = slice(first, first + size // ROWS)
+        msg[blocks] = total_sum.astype(BF16)
+        row = jnp.where(diagonal(shape, 0), top, jnp.where(diagonal(shape, ROWS), total, 0.0))
+        stat[blocks] = jnp.sum(row, axis=1, keepdims=True)
+        for group in groups:
+
+            def send(yy, group=group):
+                to = ((columns[group] + yy) * 2 + core, z)
+                for source, target, send_sem, recv_sem in ((msg, got, msend, mrecv), (stat, gotstat, ssend, srecv)):
+                    pltpu.make_async_remote_copy(
+                        src_ref=source.at[group * y_chips + yy],
+                        dst_ref=target.at[group * y_chips + y],
+                        send_sem=send_sem,
+                        recv_sem=recv_sem.at[part],
+                        device_id=to,
+                        device_id_type=MESH,
+                    ).start()
 
             if group == 0:
                 others(y_chips, y, send)
                 got[y] = msg[y]
+                gotstat[y] = stat[y]
             else:
                 for yy in range(y_chips):
                     send(yy)
 
-    for group in range(x_chips // 2):
+    group_rows = y_chips * ROWS
+    pieces = [slice(at, at + group_rows) for at in range(0, unit_rows, group_rows)]
+    tops = []
+    for group, piece in enumerate(pieces):
         await_queries(group)
-    forward(0).start()
-    _, top = turn(None, None, 0, even)
+        forward(group).start()
+        tops.append(turn(None, None, group * y_chips, even, piece=piece)[1])
+    top = jnp.concatenate(tops, axis=0)
     for group in range(x_chips // 2, x_chips):
         await_queries(group)
-    forward(1).start()
+        forward(group).start()
     copies[1].wait()
-    forward(0).wait_recv()
+    for group in range(x_chips // 2):
+        forward(group).wait_recv()
     own_first, top = turn(even, top, chips, odd)
     for which in range(3):
         own[which] = own_first[which]
-    forward(1).wait_recv()
+    for group in range(x_chips // 2, x_chips):
+        forward(group).wait_recv()
     copies[2].wait()
     copies[3].wait()
     for at in range(2):
         suffix(at)
     other, top = turn(odd, top, chips + half, even)
     give_half(0, other)
-    other, top = turn(even, top, half, odd, lambda: send_half(0, tuple(own[which] for which in range(3))))
+
+    def first_messages():
+        partials(0).wait_recv()
+        send_groups(list(range(x_chips // 2)), tuple(own[which] for which in range(3)))
+
+    other, top = turn(even, top, half, odd, first_messages)
     give_half(1, other)
-    own_second, _ = turn(odd, top, None, None)
-    send_half(1, own_second)
+    for at, piece in enumerate(pieces):
+        own_second, _ = turn(odd, top[piece], None, None, piece=piece)
+        if at == 0:
+            partials(1).wait_recv()
+        send_groups([x_chips // 2 + at], own_second)
 
     def whole(ref, count, send_sem, recv_sem):
         part = ref.at[pl.ds(0, count)]
@@ -253,13 +276,22 @@
             src_ref=part, dst_ref=part, send_sem=send_sem, recv_sem=recv_sem, device_id=(sibling, z), device_id_type=MESH
         )
 
-    whole(got, chips - 1, msend, mrecv).wait_recv()
-    sums = got[:, 0:ROWS, :].astype(F32)
-    stats = got[:, ROWS : 2 * ROWS, :].astype(F32)
-    tops = jnp.broadcast_to(stats[:, :, 0:1], sums.shape)
-    totals = jnp.broadcast_to(stats[:, :, 32:33], sums.shape) + jnp.broadcast_to(stats[:, :, 64:65], sums.shape)
-    factor = jnp.exp2(tops - jnp.max(tops, axis=0, keepdims=True))
-    result = jnp.sum(sums * factor, axis=0) / jnp.sum(totals * factor, axis=0)
+    def arrived(part):
+        count = half - 1 if part == 0 else half
+        whole(got, count, msend, mrecv.at[part]).wait_recv()
+        whole(gotstat, count, ssend, srecv.at[part]).wait_recv()
+        blocks = slice(part * half, (part + 1) * half)
+        sums = got[blocks].astype(F32)
+        stats = jnp.broadcast_to(gotstat[blocks], sums.shape)
+        tops, totals = (
+            jnp.sum(jnp.where(diagonal(sums.shape, begin), stats, 0.0), axis=2, keepdims=True) for begin in (0, ROWS)
+        )
+        top = jnp.max(tops, axis=0, keepdims=True)
+        factor = jnp.exp2(tops - top)
+        return jnp.sum(sums * factor, axis=0), jnp.sum(totals * factor, axis=0), top[0]
+
+    total_sum, total, _ = merged(arrived(0), arrived(1))
+    result = total_sum / total
     wide = [jnp.concatenate([result[at * PER_GROUP + h][None] for h in range(PER_GROUP)], axis=1) for at in range(2)]
     zbuf[z] = jnp.concatenate(wide, axis=0).astype(BF16)
 
@@ -270,11 +302,13 @@
 
     others(z_chips, z, send_result)
 
-    whole(qbuf, chips - 1, qsend, mrecv).wait_send()
+    whole(qbuf, chips - 1, qsend, zrecv).wait_send()
+    for group in range(x_chips):
+        forward(group).wait_send()
     for part in range(2):
-        forward(part).wait_send()
         partials(part).wait_send()
-    whole(msg, chips - 1, msend, mrecv).wait_send()
+    whole(msg, chips - 1, msend, zrecv).wait_send()
+    whole(stat, chips - 1, ssend, zrecv).wait_send()
     heads = whole(zbuf, z_chips - 1, zsend, zrecv)
     heads.wait_recv()
     out_ref[...] = zbuf[...]
@@ -312,18 +346,22 @@
             pltpu.VMEM((2, 2, unit_rows, HD), F32),
             pltpu.VMEM((2, 2, unit_rows, HD), F32),
             pltpu.VMEM((2, 3, ROWS, HD), F32),
-            pltpu.VMEM((chips, 2 * ROWS, HD), BF16),
-            pltpu.VMEM((chips, 2 * ROWS, HD), BF16),
+            pltpu.VMEM((chips, ROWS, HD), BF16),
+            pltpu.VMEM((chips, ROWS, HD), BF16),
+            pltpu.VMEM((chips, 1, HD), F32),
+            pltpu.VMEM((chips, 1, HD), F32),
             pltpu.VMEM((z_chips, 2, PER_GROUP * HD), BF16),
             dma((5,)),
             dma,
+            dma((x_chips,)),
+            dma((x_chips,)),
             dma((x_chips,)),
             dma((2,)),
             dma((2,)),
+            dma,
             dma((2,)),
+            dma,
             dma((2,)),
-            dma,
-            dma,
             dma,
             dma,
         ],

time: 43 us -> 41.7 us (0.970)
  Pallas kernels: 42.1 us -> 41 us
    pallas_call x1, Pallas kernels: 42.1 us -> 41 us  [on_device(): pl.pallas_call(functools.partial(attend, x_chips, y_chips, z_chips, chunk...]
where the time goes in v5:
time: 41.7 us; the launch traced here: 41.6 us
  Pallas kernels  41 us (98%)
  local copies, waits for them, and re-layouts  0.62 us (1%)
    pallas_call x1, Pallas kernels, on_device(): pl.pallas_call(functools.partial(attend, x_chips, y_chips, z_chips, chunk...  41 us

profile of v5, /device:TPU:6, one launch (start us, length us, event | category | flops | bytes accessed | tf_op | source)
XLA Modules:
  0.0 41.6 jit_solution(17481329421542977149)
XLA Ops:
  0.0 41.0 %attend.1 = bf16[8,2,1024]{2,1,0:T(2,128)(2,1)S(1)} custom-call(bf16[2,1024]{1,0:T(2,128)(2,1)} %q_ref.1, bf16[4096,128]{1,0:T(8,128)(2,1)} %pk.1, bf16[4096,128]{1,0:T(8,128)(2,1)} %pv.1, bf16[2,2048,128]{2,1,0:T(8,128)(2,1)} %sk.1, bf16[2,2048,128]{2,1,0:T(8,128)(2,1)} %sv.1, s32[2]{0:T(128)} %slen.1, s32[2]{0:T(128)} %sans.1), custom_call_target="tpu_custom_call" | custom-call | tf_op jit(solution)/shard_map/attend/pallas_call | solution.py:330
  41.0 0.6 %copy.9 = bf16[2,8192]{1,0:T(2,128)(2,1)} copy(bf16[2,8192]{1,0:T(2,128)(2,1)S(1)} %bitcast.3) | data formatting | bytes 65536

commit v6 on v5

--- a/solution.py
+++ b/solution.py
@@ -133,21 +133,32 @@
         return lax.dot_general(rows, columns, (((1,), (1,)), ((), ())), preferred_element_type=F32)
 
     def turn(now, top, begin, later, midway=None, piece=None):
-        both, later_top = None, None
         span = slice(0, unit_rows) if piece is None else piece
         size = span.stop - span.start
         rows = None if begin is None else qbuf[begin : begin + size // ROWS].reshape(size, HD)
-        for at in range(0, keys, chunk):
-            if midway is not None and at == keys // 2:
-                midway()
+
+        def step(index, carry):
+            both, later_top = carry
+            at = pl.ds(pl.multiple_of(index * chunk, chunk), chunk)
             if begin is not None:
-                scores = inner(rows, keys_here[at : at + chunk, :])
-                later[span, at : at + chunk] = scores
-                here = lane_tiles_max(scores)
-                later_top = here if later_top is None else jnp.maximum(later_top, here)
+                scores = inner(rows, keys_here[at, :])
+                later[span, at] = scores
+                later_top = jnp.maximum(later_top, lane_tiles_max(scores))
             if now is not None:
-                here = weighted(now[span, at : at + chunk], top, vbuf[at : at + chunk, :])
-                both = here if both is None else both + here
+                both = both + weighted(now[span, at], top, vbuf[at, :])
+            return both, later_top
+
+        count = keys // chunk
+        carry = (
+            None if now is None else jnp.zeros((size, 2 * HD), F32),
+            None if begin is None else jnp.full((size, HD), 10 * NEG_BIG, F32),
+        )
+        if midway is None:
+            both, later_top = lax.fori_loop(0, count, step, carry)
+        else:
+            carry = lax.fori_loop(0, count // 2, step, carry)
+            midway()
+            both, later_top = lax.fori_loop(count // 2, count, step, carry)
         part = None if now is None else (both[:, :HD], both[:, HD:], jnp.broadcast_to(top, (size, HD)))
         return part, None if begin is None else stabiliser(later_top)
 

time: 41.7 us -> 44.2 us (1.060)
  Pallas kernels: 41 us -> 43.5 us
    pallas_call x1, Pallas kernels: 41 us -> 43.5 us  [on_device(): pl.pallas_call(functools.partial(attend, x_chips, y_chips, z_chips, chunk...]
where the time goes in v6:
time: 44.2 us; the launch traced here: 44.1 us
  Pallas kernels  43.5 us (98%)
  local copies, waits for them, and re-layouts  0.62 us (1%)
    pallas_call x1, Pallas kernels, on_device(): pl.pallas_call(functools.partial(attend, x_chips, y_chips, z_chips, chunk...  43.5 us

profile of v6, /device:TPU:6, one launch (start us, length us, event | category | flops | bytes accessed | tf_op | source)
XLA Modules:
  0.0 44.1 jit_solution(16484245227804187603)
XLA Ops:
  0.0 43.5 %attend.1 = bf16[8,2,1024]{2,1,0:T(2,128)(2,1)S(1)} custom-call(bf16[2,1024]{1,0:T(2,128)(2,1)} %q_ref.1, bf16[4096,128]{1,0:T(8,128)(2,1)} %pk.1, bf16[4096,128]{1,0:T(8,128)(2,1)} %pv.1, bf16[2,2048,128]{2,1,0:T(8,128)(2,1)} %sk.1, bf16[2,2048,128]{2,1,0:T(8,128)(2,1)} %sv.1, s32[2]{0:T(128)} %slen.1, s32[2]{0:T(128)} %sans.1), custom_call_target="tpu_custom_call" | custom-call | tf_op jit(solution)/shard_map/attend/pallas_call | solution.py:341
  43.5 0.6 %copy.9 = bf16[2,8192]{1,0:T(2,128)(2,1)} copy(bf16[2,8192]{1,0:T(2,128)(2,1)S(1)} %bitcast.3) | data formatting | bytes 65536

commit v7 on v5

--- a/solution.py
+++ b/solution.py
@@ -322,7 +322,7 @@
     y_chips = chips // x_chips
     keys, cap = prefix_keys.shape[0], suffix_keys.shape[1]
     unit_rows = chips // 2 * ROWS
-    chunk = min(1024, keys)
+    chunk = min(256, keys)
     hbm = pl.BlockSpec(memory_space=pltpu.MemorySpace.HBM)
     vmem = pl.BlockSpec(memory_space=pltpu.VMEM)
     smem = pl.BlockSpec(memory_space=pltpu.SMEM)

time: 41.7 us -> 40.9 us (0.981)
  Pallas kernels: 41 us -> 40.1 us
    pallas_call x1, Pallas kernels: 41 us -> 40.1 us  [on_device(): pl.pallas_call(functools.partial(attend, x_chips, y_chips, z_chips, chunk...]
where the time goes in v7:
time: 40.9 us; the launch traced here: 40.7 us
  Pallas kernels  40.1 us (98%)
  local copies, waits for them, and re-layouts  0.62 us (2%)
    pallas_call x1, Pallas kernels, on_device(): pl.pallas_call(functools.partial(attend, x_chips, y_chips, z_chips, chunk...  40.1 us

profile of v7, /device:TPU:6, one launch (start us, length us, event | category | flops | bytes accessed | tf_op | source)
XLA Modules:
  0.0 40.7 jit_solution(13477834432776273445)
XLA Ops:
  0.0 40.1 %attend.1 = bf16[8,2,1024]{2,1,0:T(2,128)(2,1)S(1)} custom-call(bf16[2,1024]{1,0:T(2,128)(2,1)} %q_ref.1, bf16[4096,128]{1,0:T(8,128)(2,1)} %pk.1, bf16[4096,128]{1,0:T(8,128)(2,1)} %pv.1, bf16[2,2048,128]{2,1,0:T(8,128)(2,1)} %sk.1, bf16[2,2048,128]{2,1,0:T(8,128)(2,1)} %sv.1, s32[2]{0:T(128)} %slen.1, s32[2]{0:T(128)} %sans.1), custom_call_target="tpu_custom_call" | custom-call | tf_op jit(solution)/shard_map/attend/pallas_call | solution.py:330
  40.1 0.6 %copy.9 = bf16[2,8192]{1,0:T(2,128)(2,1)} copy(bf16[2,8192]{1,0:T(2,128)(2,1)S(1)} %bitcast.3) | data formatting | bytes 65536

commit v8 on v7

--- a/solution.py
+++ b/solution.py
@@ -253,9 +253,7 @@
         forward(group).wait_recv()
     copies[2].wait()
     copies[3].wait()
-    for at in range(2):
-        suffix(at)
-    other, top = turn(odd, top, chips + half, even)
+    other, top = turn(odd, top, chips + half, even, lambda: [suffix(at) for at in range(2)])
     give_half(0, other)
 
     def first_messages():

time: 40.9 us -> 41.2 us (level)
  no operation moved by 1% of the time
where the time goes in v8:
time: 41.2 us; the launch traced here: 41.1 us
  Pallas kernels  40.4 us (98%)
  local copies, waits for them, and re-layouts  0.62 us (2%)
    pallas_call x1, Pallas kernels, on_device(): pl.pallas_call(functools.partial(attend, x_chips, y_chips, z_chips, chunk...  40.4 us

profile of v8, /device:TPU:6, one launch (start us, length us, event | category | flops | bytes accessed | tf_op | source)
XLA Modules:
  0.0 41.1 jit_solution(18325624228105266830)
XLA Ops:
  0.0 40.4 %attend.1 = bf16[8,2,1024]{2,1,0:T(2,128)(2,1)S(1)} custom-call(bf16[2,1024]{1,0:T(2,128)(2,1)} %q_ref.1, bf16[4096,128]{1,0:T(8,128)(2,1)} %pk.1, bf16[4096,128]{1,0:T(8,128)(2,1)} %pv.1, bf16[2,2048,128]{2,1,0:T(8,128)(2,1)} %sk.1, bf16[2,2048,128]{2,1,0:T(8,128)(2,1)} %sv.1, s32[2]{0:T(128)} %slen.1, s32[2]{0:T(128)} %sans.1), custom_call_target="tpu_custom_call" | custom-call | tf_op jit(solution)/shard_map/attend/pallas_call | solution.py:328
  40.4 0.6 %copy.9 = bf16[2,8192]{1,0:T(2,128)(2,1)} copy(bf16[2,8192]{1,0:T(2,128)(2,1)S(1)} %bitcast.3) | data formatting | bytes 65536
